TPU v7x, 128 devices: a whole 4x4x4 slice. The times are simulated.
128 devices in a mesh: gz: 2 (over x_hi), xy: 64 (over x_lo, y, z, core).
Axes of the slice: x: 4 (x_hi: 2, x_lo: 2; x = x_hi * 2 + x_lo), y: 4, z: 4, core: 2. Of those that a mesh axis runs over, the one named last changes fastest.
Arguments:
- section_image: bfloat16 [4, 256, 2048], P('gz', 'xy'), may hold values from -6 to 6
- crack_mask: int32 [4, 256, 2048], P('gz', 'xy'), may hold values 0 or 1
- fold_mask: int32 [4, 256, 2048], P('gz', 'xy'), may hold values 0 or 1
- first_weight: bfloat16 [9, 32], replicated, may hold values from -2 to 2
- first_bias: float32 [32], replicated, may hold values from -2 to 2
- second_weight: bfloat16 [9, 32, 32], replicated, may hold values from -0.5 to 0.5
- second_bias: float32 [32], replicated, may hold values from -2 to 2
- middle_weight: bfloat16 [27, 64, 32], replicated, may hold values from -0.3125 to 0.3125
- middle_bias: float32 [64], replicated, may hold values from -2 to 2
- deeper_weight: bfloat16 [27, 64, 64], replicated, may hold values from -0.21875 to 0.21875
- deeper_bias: float32 [64], replicated, may hold values from -2 to 2
- lift_weight: bfloat16 [32, 64], replicated, may hold values from -1 to 1
- lift_bias: float32 [32], replicated, may hold values from -2 to 2
- decode_weight: bfloat16 [9, 32, 32], replicated, may hold values from -0.5 to 0.5
- decode_bias: float32 [32], replicated, may hold values from -2 to 2
- head_weight: bfloat16 [3, 32], replicated, may hold values from -1.5 to 1.5
- head_bias: float32 [3], replicated, may hold values from -2 to 2
Outputs:
- affinity: float32 [3, 4, 2048, 256], P(None, 'gz', 'xy')
All inputs are finite; a program needn't handle non-finite values. No bound on the sum of `crack_mask` or of `fold_mask` on one device may be relied on, other than what follows from the above.
Results may differ from a plain program's by a relative error of at most 0.0055.
Values may be sent and summed in bfloat16 or wider, within the bound.
A program may use at most 128 MiB of HBM per device.

v0:
```python
import jax
import jax.numpy as jnp
from jax import lax
from jax.experimental import pallas as pl
from jax.experimental.pallas import tpu as pltpu
from jax.sharding import PartitionSpec as P

BF16 = jnp.bfloat16
F32 = jnp.float32
MESH = pl.DeviceIdType.MESH
CHIPS = 32


def iota(shape, dim):
    return lax.broadcasted_iota(jnp.int32, shape, dim)


def dot(lhs, rhs):
    return jnp.dot(lhs, rhs, preferred_element_type=F32)


def dot_turned(lhs, rhs):
    return lax.dot_general(lhs, rhs, (((1,), (1,)), ((), ())), preferred_element_type=F32)


def column_of(row):
    n = row.shape[1]
    eye = iota((n, n), 0) == iota((n, n), 1)
    return jnp.sum(jnp.where(eye, row, 0.0), axis=1, keepdims=True)


def neighbours(field):
    lanes = field.shape[1]
    lane = iota(field.shape, 1)
    below = jnp.where(lane == 0, 0.0, pltpu.roll(field, 1, 1))
    above = jnp.where(lane == lanes - 1, 0.0, pltpu.roll(field, lanes - 1, 1))
    return below, field, above


def relu_plus(summed, offset, channels, low=0, high=0, keep_low=None, keep_high=None):
    rows, lanes = summed.shape
    count = rows // channels
    parts = jnp.maximum(summed.reshape(count, channels, lanes) + offset[None], 0.0)
    if low or high:
        pieces = []
        if low:
            pieces.append(parts[:low] * keep_low)
        pieces.append(parts[low : count - high])
        if high:
            pieces.append(parts[count - high :] * keep_high)
        parts = jnp.concatenate([piece for piece in pieces if piece.shape[0]], axis=0)
    return parts.reshape(rows, lanes)


def widen(piece):
    rows, lanes = piece.shape
    return jnp.concatenate([piece.astype(F32), jnp.zeros((rows, 128 - lanes), F32)], axis=1)


def plane_band(weight_ref, band_ref):
    lane = iota((32, 128), 1)
    tiles = [[None] * 5 for _ in range(4)]
    for b in range(3):
        pieces = [widen(weight_ref[3 * a + b]) for a in range(3)]
        base = pieces[0] + pltpu.roll(pieces[1], 32, 1) + pltpu.roll(pieces[2], 64, 1)
        for m in range(4):
            start = 192 * b + 32 * m
            at, off = start // 128, start % 128
            moved = pltpu.roll(base, off, 1) if off else base
            shares = [(at, moved)]
            if off + 96 > 128:
                shares = [(at, jnp.where(lane >= off, moved, 0.0)), (at + 1, jnp.where(lane < off - 32, moved, 0.0))]
            for tile, share in shares:
                old = tiles[m][tile]
                tiles[m][tile] = share if old is None else old + share
    zero = jnp.zeros((32, 128), F32)
    for m in range(4):
        row = [zero if tile is None else tile for tile in tiles[m]]
        band_ref[32 * m : 32 * m + 32, :] = jnp.concatenate(row, axis=1)[:, 0:576].astype(BF16)


def kernel(
    image_hbm, crack_hbm, fold_hbm,
    w1_hbm, b1_hbm, w2_hbm, b2_hbm, wm_hbm, bm_hbm, wd_hbm, bd_hbm, wl_hbm, bl_hbm, wc_hbm, bc_hbm, wh_hbm, bh_hbm,
    out_ref,
    image_ref, crack_ref, fold_ref,
    w1_ref, b1_ref, w2_ref, b2_ref, wm_ref, bm_ref, wd_ref, bd_ref, wl_ref, bl_ref, wc_ref, bc_ref, wh_ref, bh_ref,
    load_sem, swap_send, swap_recv, far_send, far_recv, pass_send, pass_recv,
    half, tile, strip,
    t1, t2, tm, td, tc, tl, th, stack,
    vol, one, two, joined, pooled, mid, deep, dec,
):
    gz = lax.axis_index("gz")
    xy = lax.axis_index("xy")
    core = lax.rem(xy, 2)
    chip = lax.div(xy, 2)
    last_xy = lax.axis_size("xy") - 1
    keep_low = jnp.where(xy == 0, 0.0, 1.0)
    keep_high = jnp.where(xy == last_xy, 0.0, 1.0)
    twin = (gz, xy + 1 - 2 * core)

    sources = (
        image_hbm, crack_hbm, fold_hbm,
        w1_hbm, b1_hbm, w2_hbm, b2_hbm, wm_hbm, bm_hbm, wd_hbm, bd_hbm, wl_hbm, bl_hbm, wc_hbm, bc_hbm, wh_hbm, bh_hbm,
    )
    targets = (
        image_ref, crack_ref, fold_ref,
        w1_ref, b1_ref, w2_ref, b2_ref, wm_ref, bm_ref, wd_ref, bd_ref, wl_ref, bl_ref, wc_ref, bc_ref, wh_ref, bh_ref,
    )
    loads = [pltpu.make_async_copy(s, t, load_sem.at[i]) for i, (s, t) in enumerate(zip(sources, targets))]
    for load in loads:
        load.start()

    barrier = pltpu.get_barrier_semaphore()
    pl.semaphore_signal(barrier, inc=1, device_id=twin, device_id_type=MESH)
    source_gz = jnp.where(core == 1, gz, 1 - gz)
    target_gz = jnp.where(core == 0, gz, 1 - gz)

    @pl.loop(0, CHIPS, unroll=True)
    def _(k):
        other = lax.rem(chip + k, CHIPS)
        pl.semaphore_signal(barrier, inc=1, device_id=(source_gz, 2 * other + 1 - core), device_id_type=MESH)

    for load in loads[:3]:
        load.wait()
    keep = ((1 - crack_ref[...]) * (1 - fold_ref[...])).astype(F32)
    gated = image_ref[...].astype(F32) * keep
    gated = jnp.concatenate([gated[0], gated[1]], axis=0)
    half[core] = jnp.concatenate([gated[:, :1024], gated[:, 1024:]], axis=0).astype(BF16)

    pl.semaphore_wait(barrier, CHIPS + 1)
    swap = pltpu.make_async_remote_copy(
        src_ref=half.at[core], dst_ref=half.at[core], send_sem=swap_send, recv_sem=swap_recv,
        device_id=twin, device_id_type=MESH,
    )
    swap.start()
    swap.wait()

    sub = iota((8, 128), 0)
    lane = iota((8, 128), 1)
    bands = (half[0].astype(F32), half[1].astype(F32))
    moved = []
    for q in range(2):
        evens, odds = [], []
        for k in range(16):
            rows = slice(8 * (k // 8), 8 * (k // 8) + 8)
            lanes = slice(128 * (k % 8), 128 * (k % 8) + 128)
            low, high = bands[0][rows, lanes], bands[1][rows, lanes]
            if q == 0:
                both = jnp.where(sub < 4, low, pltpu.roll(high, 4, 0))
            else:
                both = jnp.where(sub < 4, pltpu.roll(low, 4, 0), high)
            evens.append(pltpu.roll(both, 16, 1))
            odds.append(pltpu.roll(both, 80, 1))
        moved.append((evens, odds))
    for k in range(16):
        even = [jnp.where(lane >= 16, moved[q][0][k], moved[q][0][max(k - 1, 0)]) for q in range(2)]
        odd = [jnp.where(lane < 80, moved[q][1][k], moved[q][1][min(k + 1, 15)]) for q in range(2)]
        tile[2 * k] = jnp.concatenate(even, axis=0).astype(BF16)
        tile[2 * k + 1] = jnp.concatenate(odd, axis=0).astype(BF16)

    @pl.loop(0, CHIPS, unroll=True)
    def _(k):
        other = lax.rem(chip + k, CHIPS)
        pltpu.make_async_remote_copy(
            src_ref=tile.at[other], dst_ref=strip.at[0, chip], send_sem=far_send, recv_sem=far_recv,
            device_id=(target_gz, 2 * other + 1 - core), device_id_type=MESH,
        ).start()

    for load in loads[3:]:
        load.wait()
    base = [jnp.zeros((32, 128), F32), jnp.zeros((32, 128), F32)]
    lane = iota((32, 128), 1)
    w1 = w1_ref[...].astype(F32)
    for a in range(3):
        for b in range(3):
            col = column_of(w1[3 * a + b : 3 * a + b + 1])
            base[b // 2] = jnp.where(lane == 64 * (b % 2) + a, col, base[b // 2])
    for i in range(46):
        for n in range(2):
            t1[32 * i : 32 * i + 32, 128 * n : 128 * n + 128] = pltpu.roll(base[n], i, 1).astype(BF16)

    plane_band(w2_ref, t2)
    plane_band(wc_ref, tc)

    eye = (iota((64, 64), 0) == iota((64, 64), 1)).astype(BF16)
    stack[...] = jnp.zeros_like(stack)
    for e in range(3):
        place = jnp.where(gz == 0, e, 2 - e)
        for b in range(3):
            block = 3 * e + b
            for m in range(4):
                for a in range(3):
                    start = 192 * block + 32 * (m + a)
                    stack[m, start : start + 32, :] = wm_ref[9 * place + 3 * a + b]
            pieces = [widen(wd_ref[9 * place + 3 * a + b]) for a in range(3)]
            turned = [pltpu.roll(piece, 64, 1) for piece in pieces]
            rows = ((pieces[0] + turned[1], pieces[2]), (turned[0], pieces[1] + turned[2]))
            for m in range(2):
                for n in range(2):
                    start = 256 * block + 128 * n
                    td[64 * m : 64 * m + 64, start : start + 128] = rows[m][n].astype(BF16)
    for m in range(4):
        tm[64 * m : 64 * m + 64, :] = dot_turned(eye, stack[m]).astype(BF16)

    lift = widen(wl_ref[...])
    turned = pltpu.roll(lift, 64, 1)
    blank = jnp.zeros((32, 128), F32)
    for m in range(4):
        piece = turned if m % 2 else lift
        row = [piece, blank] if m < 2 else [blank, piece]
        tl[32 * m : 32 * m + 32, :] = jnp.concatenate(row, axis=1).astype(BF16)
    pick = (iota((32, 256), 0) == lax.rem(iota((32, 256), 1), 32)).astype(BF16)
    wide = dot(wh_ref[...], pick)
    row = iota((24, 256), 0)
    lane = iota((24, 256), 1)
    heads = jnp.zeros((24, 256), F32)
    for k in range(3):
        here = (row // 8 == k) & (row % 8 == lane // 32)
        heads = jnp.where(here, wide[k : k + 1], heads)
    th[...] = heads.astype(BF16)

    b1 = column_of(b1_ref[...])
    b2 = column_of(b2_ref[...])
    bm = column_of(bm_ref[...])
    bd = column_of(bd_ref[...])
    bl = column_of(bl_ref[...])
    bc = column_of(bc_ref[...])
    hrow = iota((24, 1), 0)
    bh_row = bh_ref[...]
    bh = jnp.where(hrow < 8, bh_row[:, 0:1], jnp.where(hrow < 16, bh_row[:, 1:2], bh_row[:, 2:3]))

    pltpu.make_async_copy(strip.at[0], strip.at[0], far_recv).wait()
    hand = pltpu.make_async_remote_copy(
        src_ref=strip.at[0], dst_ref=strip.at[1], send_sem=pass_send, recv_sem=pass_recv,
        device_id=twin, device_id_type=MESH,
    )
    hand.start()

    u = iota((64, 128), 0)
    l = iota((64, 128), 1)
    place = 32 * xy - 8 + u
    inside = (u < 48) & (place >= 0) & (place < 32 * (last_xy + 1))
    select = jnp.where(inside & (l == 8 + 32 * core + u), 1.0, 0.0).astype(BF16)

    for source in range(2):
        if source == 1:
            hand.wait()
        first_t = 2 * (1 - core) if source == 0 else 2 * core
        tiles = strip[source].astype(F32).reshape(CHIPS, 2, 8, 128)
        for q in range(2):
            t = first_t + jnp.where(gz == 0, q, 1 - q)
            rows = tiles[:, q].reshape(256, 128).astype(BF16)
            turned = dot_turned(select, rows)
            for b, part in enumerate(neighbours(turned)):
                vol[t, 64 * b : 64 * b + 64, :] = part.astype(BF16)
            field = vol[t]
            for chunk in range(2):
                rows = slice(736 * chunk, 736 * chunk + 736)
                found = dot(t1[rows, 0:192], field)
                if chunk == 0:
                    found = relu_plus(found, b1, 32, low=7, keep_low=keep_low)
                else:
                    found = relu_plus(found, b1, 32, high=7, keep_high=keep_high)
                for b, part in enumerate(neighbours(found)):
                    one[t, b, rows, :] = part.astype(BF16)

        @pl.loop(0, 11, unroll=True)
        def _(g):
            start = pl.multiple_of(g * 128, 128)
            halved = pl.multiple_of(g * 64, 64)
            for q in range(2):
                t = first_t + q
                field = jnp.concatenate([one[t, b, pl.ds(start, 192), :] for b in range(3)], axis=0)
                found = relu_plus(dot(t2[...], field), b2, 32)
                two[t, pl.ds(start, 128), :] = found.astype(BF16)
                pairs = found.reshape(2, 2, 32, 256)
                pairs = jnp.maximum(pairs[:, 0], pairs[:, 1]).reshape(64, 256)
                pairs = jnp.maximum(pairs, pltpu.roll(pairs, 255, 1))
                joined[t, pl.ds(halved, 64), :] = pairs.astype(BF16)

    fine = iota((256, 384), 0)
    coarse = iota((256, 384), 1)
    pick = jnp.where(fine == 2 * (coarse % 128 + coarse // 128 - 1), 1.0, 0.0).astype(BF16)
    pooled[:, :, 0:128] = jnp.zeros((3, 704, 128), BF16)
    for t in range(4):
        found = dot(joined[t], pick)
        found = jnp.concatenate([found[:96] * keep_low, found[96:608], found[608:] * keep_high], axis=0).astype(BF16)
        for b in range(3):
            pooled[b, :, 128 * (t + 1) : 128 * (t + 2)] = found[:, 128 * b : 128 * b + 128]

    mid[:, :, 0:128] = jnp.zeros((3, 1280, 128), BF16)
    for g in range(5):
        field = jnp.concatenate(
            [pooled[b, 128 * g : 128 * g + 192, 128 * e : 128 * e + 384] for e in range(3) for b in range(3)], axis=0
        )
        found = dot(tm[...], field)
        low, high = (2, 0) if g == 0 else (0, 2) if g == 4 else (0, 0)
        found = relu_plus(found, bm, 64, low, high, keep_low, keep_high)
        for t in range(3):
            for b, part in enumerate(neighbours(found[:, 128 * t : 128 * t + 128])):
                mid[b, 256 * g : 256 * g + 256, 128 * (t + 1) : 128 * (t + 2)] = part.astype(BF16)

    @pl.loop(0, 9, unroll=True)
    def _(g):
        start = pl.multiple_of(g * 128, 128)
        field = jnp.concatenate(
            [mid[b, pl.ds(start, 256), 128 * e : 128 * e + 256] for e in range(3) for b in range(3)], axis=0
        )
        deep[pl.ds(start, 128), :] = relu_plus(dot(td[...], field), bd, 64).astype(BF16)

    fine = iota((256, 256), 1)
    coarse = iota((256, 256), 0)
    double = jnp.where(fine // 2 == coarse % 128, 1.0, 0.0).astype(BF16)
    for g in range(5):
        count = 4 if g < 4 else 2
        rows = dot(tl[0 : 32 * count, 0 : 64 * count], deep[256 * g : 256 * g + 64 * count, :])
        rows = (rows.reshape(count, 32, 256) + bl[None]).reshape(32 * count, 256)
        high = rows.astype(BF16)
        low = (rows - high.astype(F32)).astype(BF16)
        for t in range(2):
            both = jnp.concatenate([high[:, 128 * t : 128 * t + 128], low[:, 128 * t : 128 * t + 128]], axis=1)
            lifted = dot(both, double)
            for r in range(count):
                for p in range(2):
                    v = 2 * (4 * g + r) + p
                    old = two[t, 32 * (v + 4) : 32 * (v + 5), :].astype(F32)
                    found = jnp.maximum(lifted[32 * r : 32 * r + 32] + old, 0.0)
                    if v < 2:
                        found = found * keep_low
                    if v >= 34:
                        found = found * keep_high
                    for b, part in enumerate(neighbours(found)):
                        dec[t, b, 32 * v : 32 * v + 32, :] = part.astype(BF16)

    @pl.loop(0, 4, unroll=True)
    def _(g):
        for t in range(2):
            parts = []
            for h in range(2):
                start = pl.multiple_of(g * 256 + 128 * h + 32, 32)
                field = jnp.concatenate([dec[t, b, pl.ds(start, 192), :] for b in range(3)], axis=0)
                parts.append(relu_plus(dot(tc[...], field), bc, 32).astype(BF16))
            logits = dot(th[...], jnp.concatenate(parts, axis=0)) + bh
            found = jax.nn.sigmoid(logits)
            s = jnp.where(gz == 0, t, 1 - t)
            for k in range(3):
                out_ref[k, s, pl.ds(pl.multiple_of(g * 8, 8), 8), :] = found[8 * k : 8 * k + 8]

    pltpu.make_async_copy(tile, tile, far_send).wait()


def body(image, crack, fold, *weights):
    rows = [weight[None] if weight.ndim == 1 else weight for weight in weights]
    rows[4] = jnp.swapaxes(rows[4], 1, 2)
    operands = (image, crack, fold, *rows)
    dma = pltpu.SemaphoreType.DMA
    scratch = [pltpu.VMEM(operand.shape, operand.dtype) for operand in operands]
    scratch += [dma((len(operands),)), dma, dma, dma, dma, dma, dma]
    scratch += [
        pltpu.VMEM(shape, BF16)
        for shape in (
            (2, 16, 1024), (CHIPS, 16, 128), (2, CHIPS, 16, 128),
            (1472, 256), (128, 576), (256, 1728), (128, 2304), (128, 576), (128, 256), (24, 256), (4, 1728, 64),
            (4, 192, 256), (4, 3, 1472, 256), (4, 1408, 256), (4, 704, 256), (3, 704, 640), (3, 1280, 512),
            (1152, 256), (2, 3, 1152, 256),
        )
    ]
    return pl.pallas_call(
        kernel,
        out_shape=jax.ShapeDtypeStruct((3, 2, 32, 256), F32),
        in_specs=[pl.BlockSpec(memory_space=pl.ANY)] * len(operands),
        out_specs=pl.BlockSpec(memory_space=pltpu.VMEM),
        scratch_shapes=scratch,
        compiler_params=pltpu.CompilerParams(
            collective_id=0, has_side_effects=True, vmem_limit_bytes=60 * 1024 * 1024
        ),
        name="window",
    )(*operands)


def solution(mesh):
    in_specs = (P("gz", "xy", None),) * 3 + (P(),) * 14
    out_specs = P(None, "gz", "xy", None)
    return jax.shard_map(body, mesh=mesh, in_specs=in_specs, out_specs=out_specs, check_vma=False)
```

profile of v0, /device:TPU:1, one launch (start us, length us, event | category | flops | bytes accessed | tf_op | source)
XLA Modules:
  0.0 32.9 jit_solution(8057958540917967866)
XLA Ops:
  0.0 31.3 %window.1 = f32[3,2,32,256]{3,2,1,0:T(8,128)} custom-call(bf16[2,4,2048]{2,1,0:T(4,128)(2,1)} %image_hbm.1, s32[2,4,2048]{2,1,0:T(4,128)} %crack_hbm.1, s32[2,4,2048]{2,1,0:T(4,128)} %fold_hbm.1, bf16[9,32]{1,0:T(8,128)(2,1)} %w1_hbm.1, f32[1,32]{1,0:T(1,128)} %bitcast.9, bf16[9,32,32]{2,1,0:T(8,128)(2,1)} %w2_hbm.1, f32[1,32]{1,0:T(1,128)} %bitcast.10, ...), custom_call_target="tpu_custom_call" | custom-call | tf_op jit(solution)/shard_map/window/pallas_call | solution.py:369
  31.3 1.6 %copy.19 = f32[3,2,32,256]{3,2,1,0:T(8,128)} copy(f32[3,2,32,256]{3,2,1,0:T(8,128)} %window.1) | data formatting | bytes 393216
where the time goes:
time: 33.1 us; the launch traced here: 32.9 us
  Pallas kernels  31.3 us (95%)
  local copies, waits for them, and re-layouts  1.62 us (5%)
    pallas_call x1, Pallas kernels, body(): pl.pallas_call(kernel, out_shape=jax.ShapeDtypeStruct((3, 2, 32, 256), F3...  31.3 us
    unnamed x1, local copies, waits for them, and re-layouts  1.62 us

commit v1 on v0

--- a/solution.py
+++ b/solution.py
@@ -50,6 +50,22 @@
             pieces.append(parts[count - high :] * keep_high)
         parts = jnp.concatenate([piece for piece in pieces if piece.shape[0]], axis=0)
     return parts.reshape(rows, lanes)
+
+
+def gather_rows(summed, channels):
+    rows, lanes = summed.shape
+    taps = summed.reshape(rows // (3 * channels), 3, channels, lanes)
+    below, here, above = (taps[:, b].reshape(rows // 3, lanes) for b in range(3))
+    lane = iota((rows // 3, 128), 1)
+    parts = []
+    for n in range(lanes // 128):
+        block = slice(128 * n, 128 * n + 128)
+        parts.append(
+            here[:, block]
+            + jnp.where(lane == 0, 0.0, pltpu.roll(below[:, block], 1, 1))
+            + jnp.where(lane == 127, 0.0, pltpu.roll(above[:, block], 127, 1))
+        )
+    return jnp.concatenate(parts, axis=1)
 
 
 def widen(piece):
@@ -87,7 +103,7 @@
     w1_ref, b1_ref, w2_ref, b2_ref, wm_ref, bm_ref, wd_ref, bd_ref, wl_ref, bl_ref, wc_ref, bc_ref, wh_ref, bh_ref,
     load_sem, swap_send, swap_recv, far_send, far_recv, pass_send, pass_recv,
     half, tile, strip,
-    t1, t2, tm, td, tc, tl, th, stack,
+    t1, t2, tm, td, tc, tl, th,
     vol, one, two, joined, pooled, mid, deep, dec,
 ):
     gz = lax.axis_index("gz")
@@ -98,6 +114,11 @@
     keep_low = jnp.where(xy == 0, 0.0, 1.0)
     keep_high = jnp.where(xy == last_xy, 0.0, 1.0)
     twin = (gz, xy + 1 - 2 * core)
+
+    x, y, z = lax.div(chip, 16), lax.rem(lax.div(chip, 4), 4), lax.rem(chip, 4)
+    steps = [(i, j, k) for i in range(2) for j in range(4) for k in range(4)]
+    steps.sort(key=lambda step: -(2 - abs(2 - step[1]) + 2 - abs(2 - step[2])))
+    others = [16 * lax.rem(x + i, 2) + 4 * lax.rem(y + j, 4) + lax.rem(z + k, 4) for i, j, k in steps]
 
     sources = (
         image_hbm, crack_hbm, fold_hbm,
@@ -116,9 +137,7 @@
     source_gz = jnp.where(core == 1, gz, 1 - gz)
     target_gz = jnp.where(core == 0, gz, 1 - gz)
 
-    @pl.loop(0, CHIPS, unroll=True)
-    def _(k):
-        other = lax.rem(chip + k, CHIPS)
+    for other in others:
         pl.semaphore_signal(barrier, inc=1, device_id=(source_gz, 2 * other + 1 - core), device_id_type=MESH)
 
     for load in loads[:3]:
@@ -159,9 +178,7 @@
         tile[2 * k] = jnp.concatenate(even, axis=0).astype(BF16)
         tile[2 * k + 1] = jnp.concatenate(odd, axis=0).astype(BF16)
 
-    @pl.loop(0, CHIPS, unroll=True)
-    def _(k):
-        other = lax.rem(chip + k, CHIPS)
+    for other in others:
         pltpu.make_async_remote_copy(
             src_ref=tile.at[other], dst_ref=strip.at[0, chip], send_sem=far_send, recv_sem=far_recv,
             device_id=(target_gz, 2 * other + 1 - core), device_id_type=MESH,
@@ -184,24 +201,22 @@
     plane_band(wc_ref, tc)
 
     eye = (iota((64, 64), 0) == iota((64, 64), 1)).astype(BF16)
-    stack[...] = jnp.zeros_like(stack)
     for e in range(3):
         place = jnp.where(gz == 0, e, 2 - e)
         for b in range(3):
-            block = 3 * e + b
-            for m in range(4):
-                for a in range(3):
-                    start = 192 * block + 32 * (m + a)
-                    stack[m, start : start + 32, :] = wm_ref[9 * place + 3 * a + b]
+            rows = [wm_ref[9 * place + 3 * a + b] for a in range(3)]
+            base = dot_turned(eye, jnp.concatenate([*rows, jnp.zeros((32, 64), BF16)], axis=0))
+            for m in range(2):
+                moved = pltpu.roll(base, 32, 1) if m else base
+                start = 192 * m + 64 * b
+                tm[start : start + 64, 128 * e : 128 * e + 128] = moved.astype(BF16)
             pieces = [widen(wd_ref[9 * place + 3 * a + b]) for a in range(3)]
             turned = [pltpu.roll(piece, 64, 1) for piece in pieces]
             rows = ((pieces[0] + turned[1], pieces[2]), (turned[0], pieces[1] + turned[2]))
             for m in range(2):
+                start = 192 * m + 64 * b
                 for n in range(2):
-                    start = 256 * block + 128 * n
-                    td[64 * m : 64 * m + 64, start : start + 128] = rows[m][n].astype(BF16)
-    for m in range(4):
-        tm[64 * m : 64 * m + 64, :] = dot_turned(eye, stack[m]).astype(BF16)
+                    td[start : start + 64, 256 * e + 128 * n : 256 * e + 128 * n + 128] = rows[m][n].astype(BF16)
 
     lift = widen(wl_ref[...])
     turned = pltpu.roll(lift, 64, 1)
@@ -279,35 +294,35 @@
                 pairs = jnp.maximum(pairs, pltpu.roll(pairs, 255, 1))
                 joined[t, pl.ds(halved, 64), :] = pairs.astype(BF16)
 
-    fine = iota((256, 384), 0)
-    coarse = iota((256, 384), 1)
-    pick = jnp.where(fine == 2 * (coarse % 128 + coarse // 128 - 1), 1.0, 0.0).astype(BF16)
-    pooled[:, :, 0:128] = jnp.zeros((3, 704, 128), BF16)
+    fine = iota((256, 128), 0)
+    coarse = iota((256, 128), 1)
+    pick = jnp.where(fine == 2 * coarse, 1.0, 0.0).astype(BF16)
+    pooled[:, 0:128] = jnp.zeros((704, 128), BF16)
     for t in range(4):
         found = dot(joined[t], pick)
         found = jnp.concatenate([found[:96] * keep_low, found[96:608], found[608:] * keep_high], axis=0).astype(BF16)
-        for b in range(3):
-            pooled[b, :, 128 * (t + 1) : 128 * (t + 2)] = found[:, 128 * b : 128 * b + 128]
-
-    mid[:, :, 0:128] = jnp.zeros((3, 1280, 128), BF16)
+        pooled[:, 128 * (t + 1) : 128 * (t + 2)] = found
+
+    mid[:, 0:128] = jnp.zeros((1280, 128), BF16)
     for g in range(5):
-        field = jnp.concatenate(
-            [pooled[b, 128 * g : 128 * g + 192, 128 * e : 128 * e + 384] for e in range(3) for b in range(3)], axis=0
-        )
-        found = dot(tm[...], field)
-        low, high = (2, 0) if g == 0 else (0, 2) if g == 4 else (0, 0)
-        found = relu_plus(found, bm, 64, low, high, keep_low, keep_high)
-        for t in range(3):
-            for b, part in enumerate(neighbours(found[:, 128 * t : 128 * t + 128])):
-                mid[b, 256 * g : 256 * g + 256, 128 * (t + 1) : 128 * (t + 2)] = part.astype(BF16)
-
-    @pl.loop(0, 9, unroll=True)
-    def _(g):
-        start = pl.multiple_of(g * 128, 128)
-        field = jnp.concatenate(
-            [mid[b, pl.ds(start, 256), 128 * e : 128 * e + 256] for e in range(3) for b in range(3)], axis=0
-        )
-        deep[pl.ds(start, 128), :] = relu_plus(dot(td[...], field), bd, 64).astype(BF16)
+        field = []
+        for e in range(3):
+            near = [pooled[128 * g + 64 * h : 128 * g + 64 * h + 128, 128 * e : 128 * e + 384] for h in range(2)]
+            field.append(jnp.concatenate([near[0][:, :256], near[1][:, :256], near[0][:, 256:], near[1][:, 256:]], axis=1))
+        found = gather_rows(dot(tm[...], jnp.concatenate(field, axis=0)), 64)
+        found = jnp.maximum(found.reshape(2, 64, 768) + bm[None], 0.0).reshape(128, 768)
+        for h in range(2):
+            part = jnp.concatenate([found[:, 256 * h : 256 * h + 256], found[:, 512 + 128 * h : 640 + 128 * h]], axis=1)
+            if g == 0 and h == 0:
+                part = part * keep_low
+            if g == 4 and h == 1:
+                part = part * keep_high
+            mid[256 * g + 128 * h : 256 * g + 128 * h + 128, 128:512] = part.astype(BF16)
+
+    for g in range(9):
+        field = jnp.concatenate([mid[128 * g : 128 * g + 256, 128 * e : 128 * e + 256] for e in range(3)], axis=0)
+        found = gather_rows(dot(td[...], field), 64)
+        deep[128 * g : 128 * g + 128, :] = jnp.maximum(found.reshape(2, 64, 256) + bd[None], 0.0).reshape(128, 256).astype(BF16)
 
     fine = iota((256, 256), 1)
     coarse = iota((256, 256), 0)
@@ -361,8 +376,8 @@
         pltpu.VMEM(shape, BF16)
         for shape in (
             (2, 16, 1024), (CHIPS, 16, 128), (2, CHIPS, 16, 128),
-            (1472, 256), (128, 576), (256, 1728), (128, 2304), (128, 576), (128, 256), (24, 256), (4, 1728, 64),
-            (4, 192, 256), (4, 3, 1472, 256), (4, 1408, 256), (4, 704, 256), (3, 704, 640), (3, 1280, 512),
+            (1472, 256), (128, 576), (384, 384), (384, 768), (128, 576), (128, 256), (24, 256),
+            (4, 192, 256), (4, 3, 1472, 256), (4, 1408, 256), (4, 704, 256), (704, 640), (1280, 512),
             (1152, 256), (2, 3, 1152, 256),
         )
     ]

time: 33.1 us -> 31.4 us (0.949)
  Pallas kernels: 31.3 us -> 29.7 us
    pallas_call x1, Pallas kernels: 31.3 us -> 29.7 us  [body(): pl.pallas_call(kernel, out_shape=jax.ShapeDtypeStruct((3, 2, 32, 256), F3...]
where the time goes in v1:
time: 31.4 us; the launch traced here: 31.3 us
  Pallas kernels  29.7 us (95%)
  local copies, waits for them, and re-layouts  1.62 us (5%)
    pallas_call x1, Pallas kernels, body(): pl.pallas_call(kernel, out_shape=jax.ShapeDtypeStruct((3, 2, 32, 256), F3...  29.7 us
    unnamed x1, local copies, waits for them, and re-layouts  1.62 us

profile of v1, /device:TPU:1, one launch (start us, length us, event | category | flops | bytes accessed | tf_op | source)
XLA Modules:
  0.0 31.3 jit_solution(8469225272548864920)
XLA Ops:
  0.0 29.7 %window.1 = f32[3,2,32,256]{3,2,1,0:T(8,128)} custom-call(bf16[2,4,2048]{2,1,0:T(4,128)(2,1)} %image_hbm.1, s32[2,4,2048]{2,1,0:T(4,128)} %crack_hbm.1, s32[2,4,2048]{2,1,0:T(4,128)} %fold_hbm.1, bf16[9,32]{1,0:T(8,128)(2,1)} %w1_hbm.1, f32[1,32]{1,0:T(1,128)} %bitcast.9, bf16[9,32,32]{2,1,0:T(8,128)(2,1)} %w2_hbm.1, f32[1,32]{1,0:T(1,128)} %bitcast.10, ...), custom_call_target="tpu_custom_call" | custom-call | tf_op jit(solution)/shard_map/window/pallas_call | solution.py:384
  29.7 1.6 %copy.19 = f32[3,2,32,256]{3,2,1,0:T(8,128)} copy(f32[3,2,32,256]{3,2,1,0:T(8,128)} %window.1) | data formatting | bytes 393216

commit v2 on v1

--- a/solution.py
+++ b/solution.py
@@ -261,47 +261,42 @@
     for source in range(2):
         if source == 1:
             hand.wait()
-        first_t = 2 * (1 - core) if source == 0 else 2 * core
         tiles = strip[source].astype(F32).reshape(CHIPS, 2, 8, 128)
         for q in range(2):
-            t = first_t + jnp.where(gz == 0, q, 1 - q)
+            p = 2 * source + q
             rows = tiles[:, q].reshape(256, 128).astype(BF16)
             turned = dot_turned(select, rows)
             for b, part in enumerate(neighbours(turned)):
-                vol[t, 64 * b : 64 * b + 64, :] = part.astype(BF16)
-            field = vol[t]
+                vol[p, 64 * b : 64 * b + 64, :] = part.astype(BF16)
             for chunk in range(2):
                 rows = slice(736 * chunk, 736 * chunk + 736)
-                found = dot(t1[rows, 0:192], field)
+                found = dot(t1[rows, 0:192], vol[p])
                 if chunk == 0:
                     found = relu_plus(found, b1, 32, low=7, keep_low=keep_low)
                 else:
                     found = relu_plus(found, b1, 32, high=7, keep_high=keep_high)
                 for b, part in enumerate(neighbours(found)):
-                    one[t, b, rows, :] = part.astype(BF16)
-
-        @pl.loop(0, 11, unroll=True)
-        def _(g):
-            start = pl.multiple_of(g * 128, 128)
-            halved = pl.multiple_of(g * 64, 64)
+                    one[p, b, rows, :] = part.astype(BF16)
+        for g in range(11):
             for q in range(2):
-                t = first_t + q
-                field = jnp.concatenate([one[t, b, pl.ds(start, 192), :] for b in range(3)], axis=0)
+                p = 2 * source + q
+                field = jnp.concatenate([one[p, b, 128 * g : 128 * g + 192, :] for b in range(3)], axis=0)
                 found = relu_plus(dot(t2[...], field), b2, 32)
-                two[t, pl.ds(start, 128), :] = found.astype(BF16)
+                two[p, 128 * g : 128 * g + 128, :] = found.astype(BF16)
                 pairs = found.reshape(2, 2, 32, 256)
                 pairs = jnp.maximum(pairs[:, 0], pairs[:, 1]).reshape(64, 256)
                 pairs = jnp.maximum(pairs, pltpu.roll(pairs, 255, 1))
-                joined[t, pl.ds(halved, 64), :] = pairs.astype(BF16)
+                joined[p, 64 * g : 64 * g + 64, :] = pairs.astype(BF16)
 
     fine = iota((256, 128), 0)
     coarse = iota((256, 128), 1)
     pick = jnp.where(fine == 2 * coarse, 1.0, 0.0).astype(BF16)
     pooled[:, 0:128] = jnp.zeros((704, 128), BF16)
-    for t in range(4):
-        found = dot(joined[t], pick)
+    for p in range(4):
+        found = dot(joined[p], pick)
         found = jnp.concatenate([found[:96] * keep_low, found[96:608], found[608:] * keep_high], axis=0).astype(BF16)
-        pooled[:, 128 * (t + 1) : 128 * (t + 2)] = found
+        t = jnp.where(core == 1, 2 * (p // 2), 2 - 2 * (p // 2)) + jnp.where(gz == 0, p % 2, 1 - p % 2)
+        pooled[:, pl.ds(pl.multiple_of(128 * (t + 1), 128), 128)] = found
 
     mid[:, 0:128] = jnp.zeros((1280, 128), BF16)
     for g in range(5):
@@ -339,7 +334,8 @@
             for r in range(count):
                 for p in range(2):
                     v = 2 * (4 * g + r) + p
-                    old = two[t, 32 * (v + 4) : 32 * (v + 5), :].astype(F32)
+                    p = jnp.where(core == 1, 0, 2) + jnp.where(gz == 0, t, 1 - t)
+                    old = two[p, 32 * (v + 4) : 32 * (v + 5), :].astype(F32)
                     found = jnp.maximum(lifted[32 * r : 32 * r + 32] + old, 0.0)
                     if v < 2:
                         found = found * keep_low
@@ -348,19 +344,18 @@
                     for b, part in enumerate(neighbours(found)):
                         dec[t, b, 32 * v : 32 * v + 32, :] = part.astype(BF16)
 
-    @pl.loop(0, 4, unroll=True)
-    def _(g):
+    for g in range(4):
         for t in range(2):
             parts = []
             for h in range(2):
-                start = pl.multiple_of(g * 256 + 128 * h + 32, 32)
-                field = jnp.concatenate([dec[t, b, pl.ds(start, 192), :] for b in range(3)], axis=0)
+                start = g * 256 + 128 * h + 32
+                field = jnp.concatenate([dec[t, b, start : start + 192, :] for b in range(3)], axis=0)
                 parts.append(relu_plus(dot(tc[...], field), bc, 32).astype(BF16))
             logits = dot(th[...], jnp.concatenate(parts, axis=0)) + bh
             found = jax.nn.sigmoid(logits)
             s = jnp.where(gz == 0, t, 1 - t)
             for k in range(3):
-                out_ref[k, s, pl.ds(pl.multiple_of(g * 8, 8), 8), :] = found[8 * k : 8 * k + 8]
+                out_ref[k, s, 8 * g : 8 * g + 8, :] = found[8 * k : 8 * k + 8]
 
     pltpu.make_async_copy(tile, tile, far_send).wait()
 
@@ -383,7 +378,7 @@
     ]
     return pl.pallas_call(
         kernel,
-        out_shape=jax.ShapeDtypeStruct((3, 2, 32, 256), F32),
+        out_shape=pltpu.VMEM((3, 2, 32, 256), F32),
         in_specs=[pl.BlockSpec(memory_space=pl.ANY)] * len(operands),
         out_specs=pl.BlockSpec(memory_space=pltpu.VMEM),
         scratch_shapes=scratch,

time: 31.4 us -> 27.9 us (0.89)
  Pallas kernels: 29.7 us -> 27.1 us
  local copies, waits for them, and re-layouts: 1.62 us -> 0.68 us
    pallas_call x1, Pallas kernels: 29.7 us -> 27.1 us  [body(): pl.pallas_call(kernel, out_shape=pltpu.VMEM((3, 2, 32, 256), F32), in_spe...]
    unnamed x1, local copies, waits for them, and re-layouts: 1.62 us -> 0.68 us
where the time goes in v2:
time: 27.9 us; the launch traced here: 27.8 us
  Pallas kernels  27.1 us (97%)
  local copies, waits for them, and re-layouts  0.68 us (2%)
    pallas_call x1, Pallas kernels, body(): pl.pallas_call(kernel, out_shape=pltpu.VMEM((3, 2, 32, 256), F32), in_spe...  27.1 us
    unnamed x1, local copies, waits for them, and re-layouts  0.68 us

profile of v2, /device:TPU:1, one launch (start us, length us, event | category | flops | bytes accessed | tf_op | source)
XLA Modules:
  0.0 27.8 jit_solution(7287763458666720974)
XLA Ops:
  0.0 27.1 %window.1 = f32[3,2,32,256]{3,2,1,0:T(8,128)S(1)} custom-call(bf16[2,4,2048]{2,1,0:T(4,128)(2,1)} %image_hbm.1, s32[2,4,2048]{2,1,0:T(4,128)} %crack_hbm.1, s32[2,4,2048]{2,1,0:T(4,128)} %fold_hbm.1, bf16[9,32]{1,0:T(8,128)(2,1)} %w1_hbm.1, f32[1,32]{1,0:T(1,128)} %bitcast.9, bf16[9,32,32]{2,1,0:T(8,128)(2,1)} %w2_hbm.1, f32[1,32]{1,0:T(1,128)} %bitcast.10, ...), custom_call_target="tpu_custom_call" | custom-call | tf_op jit(solution)/shard_map/window/pallas_call | solution.py:379
  27.1 0.7 %copy.19 = f32[3,2,32,256]{3,2,1,0:T(8,128)} copy(f32[3,2,32,256]{3,2,1,0:T(8,128)S(1)} %window.1) | data formatting | bytes 393216

commit v3 on v2

--- a/solution.py
+++ b/solution.py
@@ -104,7 +104,7 @@
     load_sem, swap_send, swap_recv, far_send, far_recv, pass_send, pass_recv,
     half, tile, strip,
     t1, t2, tm, td, tc, tl, th,
-    vol, one, two, joined, pooled, mid, deep, dec,
+    vol, one, two, joined, pooled, mid, deep, lifts, dec,
 ):
     gz = lax.axis_index("gz")
     xy = lax.axis_index("xy")
@@ -118,7 +118,7 @@
     x, y, z = lax.div(chip, 16), lax.rem(lax.div(chip, 4), 4), lax.rem(chip, 4)
     steps = [(i, j, k) for i in range(2) for j in range(4) for k in range(4)]
     steps.sort(key=lambda step: -(2 - abs(2 - step[1]) + 2 - abs(2 - step[2])))
-    others = [16 * lax.rem(x + i, 2) + 4 * lax.rem(y + j, 4) + lax.rem(z + k, 4) for i, j, k in steps]
+    others = [16 * lax.rem(x + i + 1 - core, 2) + 4 * lax.rem(y + j, 4) + lax.rem(z + k, 4) for i, j, k in steps]
 
     sources = (
         image_hbm, crack_hbm, fold_hbm,
@@ -129,7 +129,7 @@
         w1_ref, b1_ref, w2_ref, b2_ref, wm_ref, bm_ref, wd_ref, bd_ref, wl_ref, bl_ref, wc_ref, bc_ref, wh_ref, bh_ref,
     )
     loads = [pltpu.make_async_copy(s, t, load_sem.at[i]) for i, (s, t) in enumerate(zip(sources, targets))]
-    for load in loads:
+    for load in loads[:3]:
         load.start()
 
     barrier = pltpu.get_barrier_semaphore()
@@ -153,6 +153,8 @@
         device_id=twin, device_id_type=MESH,
     )
     swap.start()
+    for load in loads[3:]:
+        load.start()
     swap.wait()
 
     sub = iota((8, 128), 0)
@@ -291,37 +293,56 @@
     fine = iota((256, 128), 0)
     coarse = iota((256, 128), 1)
     pick = jnp.where(fine == 2 * coarse, 1.0, 0.0).astype(BF16)
-    pooled[:, 0:128] = jnp.zeros((704, 128), BF16)
     for p in range(4):
         found = dot(joined[p], pick)
         found = jnp.concatenate([found[:96] * keep_low, found[96:608], found[608:] * keep_high], axis=0).astype(BF16)
         t = jnp.where(core == 1, 2 * (p // 2), 2 - 2 * (p // 2)) + jnp.where(gz == 0, p % 2, 1 - p % 2)
         pooled[:, pl.ds(pl.multiple_of(128 * (t + 1), 128), 128)] = found
 
-    mid[:, 0:128] = jnp.zeros((1280, 128), BF16)
+    mid[1024:1280, 0:128] = jnp.zeros((256, 128), BF16)
     for g in range(5):
-        field = []
-        for e in range(3):
-            near = [pooled[128 * g + 64 * h : 128 * g + 64 * h + 128, 128 * e : 128 * e + 384] for h in range(2)]
-            field.append(jnp.concatenate([near[0][:, :256], near[1][:, :256], near[0][:, 256:], near[1][:, 256:]], axis=1))
-        found = gather_rows(dot(tm[...], jnp.concatenate(field, axis=0)), 64)
-        found = jnp.maximum(found.reshape(2, 64, 768) + bm[None], 0.0).reshape(128, 768)
+        rows = [slice(128 * g + 64 * h, 128 * g + 64 * h + 128) for h in range(2)]
+        field = [jnp.concatenate([pooled[rows[h], 128 * e : 128 * e + 128] for h in range(2)], axis=1) for e in (1, 2)]
+        sums = [dot(tm[:, 128:384], jnp.concatenate(field, axis=0))]
         for h in range(2):
-            part = jnp.concatenate([found[:, 256 * h : 256 * h + 256], found[:, 512 + 128 * h : 640 + 128 * h]], axis=1)
-            if g == 0 and h == 0:
-                part = part * keep_low
-            if g == 4 and h == 1:
-                part = part * keep_high
-            mid[256 * g + 128 * h : 256 * g + 128 * h + 128, 128:512] = part.astype(BF16)
-
-    for g in range(9):
-        field = jnp.concatenate([mid[128 * g : 128 * g + 256, 128 * e : 128 * e + 256] for e in range(3)], axis=0)
-        found = gather_rows(dot(td[...], field), 64)
-        deep[128 * g : 128 * g + 128, :] = jnp.maximum(found.reshape(2, 64, 256) + bd[None], 0.0).reshape(128, 256).astype(BF16)
-
-    fine = iota((256, 256), 1)
-    coarse = iota((256, 256), 0)
-    double = jnp.where(fine // 2 == coarse % 128, 1.0, 0.0).astype(BF16)
+            field = [pooled[rows[h], 128 * e + 128 : 128 * e + 384] for e in range(3)]
+            sums.append(dot(tm[...], jnp.concatenate(field, axis=0)))
+        found = []
+        for summed in sums:
+            summed = gather_rows(summed, 64)
+            found.append(jnp.maximum(summed.reshape(2, 64, 256) + bm[None], 0.0).reshape(128, 256))
+        for h in range(2):
+            scale = keep_low if g == 0 and h == 0 else keep_high if g == 4 and h == 1 else None
+            start = 256 * g + 128 * h
+            for part, lanes in ((found[0][:, 128 * h : 128 * h + 128], slice(128, 256)), (found[1 + h], slice(256, 512))):
+                if scale is not None:
+                    part = part * scale
+                mid[start : start + 128, lanes] = part.astype(BF16)
+
+    for g in range(0, 9, 2):
+        rows = [slice(128 * i, 128 * i + 256) for i in (g, g + 1)]
+        if g < 8:
+            sums = []
+            for t in range(2):
+                field = [
+                    jnp.concatenate([mid[row, 128 * (e + t) : 128 * (e + t) + 128] for row in rows], axis=1)
+                    for e in range(1 - t, 3)
+                ]
+                sums.append(dot(td[:, 256 * (1 - t) : 768], jnp.concatenate(field, axis=0)))
+        else:
+            sums = [dot(td[...], jnp.concatenate([mid[rows[0], 128 * e : 128 * e + 256] for e in range(3)], axis=0))]
+        found = []
+        for summed in sums:
+            summed = gather_rows(summed, 64)
+            found.append(jnp.maximum(summed.reshape(2, 64, 256) + bd[None], 0.0).reshape(128, 256).astype(BF16))
+        if g < 8:
+            for i in range(2):
+                start = 128 * (g + i)
+                for t in range(2):
+                    deep[start : start + 128, 128 * t : 128 * t + 128] = found[t][:, 128 * i : 128 * i + 128]
+        else:
+            deep[1024:1152, :] = found[0]
+
     for g in range(5):
         count = 4 if g < 4 else 2
         rows = dot(tl[0 : 32 * count, 0 : 64 * count], deep[256 * g : 256 * g + 64 * count, :])
@@ -330,11 +351,19 @@
         low = (rows - high.astype(F32)).astype(BF16)
         for t in range(2):
             both = jnp.concatenate([high[:, 128 * t : 128 * t + 128], low[:, 128 * t : 128 * t + 128]], axis=1)
-            lifted = dot(both, double)
+            lifts[t, 128 * g : 128 * g + 32 * count, :] = both
+
+    fine = iota((256, 256), 1)
+    coarse = iota((256, 256), 0)
+    double = jnp.where(fine // 2 == coarse % 128, 1.0, 0.0).astype(BF16)
+    for g in range(5):
+        count = 4 if g < 4 else 2
+        for t in range(2):
+            lifted = dot(lifts[t, 128 * g : 128 * g + 32 * count, :], double)
+            p = jnp.where(core == 1, 0, 2) + jnp.where(gz == 0, t, 1 - t)
             for r in range(count):
-                for p in range(2):
-                    v = 2 * (4 * g + r) + p
-                    p = jnp.where(core == 1, 0, 2) + jnp.where(gz == 0, t, 1 - t)
+                for q in range(2):
+                    v = 2 * (4 * g + r) + q
                     old = two[p, 32 * (v + 4) : 32 * (v + 5), :].astype(F32)
                     found = jnp.maximum(lifted[32 * r : 32 * r + 32] + old, 0.0)
                     if v < 2:
@@ -344,15 +373,20 @@
                     for b, part in enumerate(neighbours(found)):
                         dec[t, b, 32 * v : 32 * v + 32, :] = part.astype(BF16)
 
-    for g in range(4):
-        for t in range(2):
+    steps = [(g, t) for g in range(4) for t in range(2)]
+    fields = []
+    for step in range(len(steps) + 2):
+        if step < len(steps):
+            g, t = steps[step]
             parts = []
             for h in range(2):
                 start = g * 256 + 128 * h + 32
                 field = jnp.concatenate([dec[t, b, start : start + 192, :] for b in range(3)], axis=0)
                 parts.append(relu_plus(dot(tc[...], field), bc, 32).astype(BF16))
-            logits = dot(th[...], jnp.concatenate(parts, axis=0)) + bh
-            found = jax.nn.sigmoid(logits)
+            fields.append(jnp.concatenate(parts, axis=0))
+        if step >= 2:
+            g, t = steps[step - 2]
+            found = jax.nn.sigmoid(dot(th[...], fields[step - 2]) + bh)
             s = jnp.where(gz == 0, t, 1 - t)
             for k in range(3):
                 out_ref[k, s, 8 * g : 8 * g + 8, :] = found[8 * k : 8 * k + 8]
@@ -373,7 +407,7 @@
             (2, 16, 1024), (CHIPS, 16, 128), (2, CHIPS, 16, 128),
             (1472, 256), (128, 576), (384, 384), (384, 768), (128, 576), (128, 256), (24, 256),
             (4, 192, 256), (4, 3, 1472, 256), (4, 1408, 256), (4, 704, 256), (704, 640), (1280, 512),
-            (1152, 256), (2, 3, 1152, 256),
+            (1152, 256), (2, 576, 256), (2, 3, 1152, 256),
         )
     ]
     return pl.pallas_call(

time: 27.9 us -> 26.5 us (0.950)
  Pallas kernels: 27.1 us -> 25.6 us
    pallas_call x1, Pallas kernels: 27.1 us -> 25.6 us  [body(): pl.pallas_call(kernel, out_shape=pltpu.VMEM((3, 2, 32, 256), F32), in_spe...]
where the time goes in v3:
time: 26.5 us; the launch traced here: 26.3 us
  Pallas kernels  25.6 us (97%)
  local copies, waits for them, and re-layouts  0.68 us (3%)
    pallas_call x1, Pallas kernels, body(): pl.pallas_call(kernel, out_shape=pltpu.VMEM((3, 2, 32, 256), F32), in_spe...  25.6 us
    unnamed x1, local copies, waits for them, and re-layouts  0.68 us

profile of v3, /device:TPU:1, one launch (start us, length us, event | category | flops | bytes accessed | tf_op | source)
XLA Modules:
  0.0 26.3 jit_solution(5316355598495847769)
XLA Ops:
  0.0 25.6 %window.1 = f32[3,2,32,256]{3,2,1,0:T(8,128)S(1)} custom-call(bf16[2,4,2048]{2,1,0:T(4,128)(2,1)} %image_hbm.1, s32[2,4,2048]{2,1,0:T(4,128)} %crack_hbm.1, s32[2,4,2048]{2,1,0:T(4,128)} %fold_hbm.1, bf16[9,32]{1,0:T(8,128)(2,1)} %w1_hbm.1, f32[1,32]{1,0:T(1,128)} %bitcast.9, bf16[9,32,32]{2,1,0:T(8,128)(2,1)} %w2_hbm.1, f32[1,32]{1,0:T(1,128)} %bitcast.10, ...), custom_call_target="tpu_custom_call" | custom-call | tf_op jit(solution)/shard_map/window/pallas_call | solution.py:413
  25.6 0.7 %copy.19 = f32[3,2,32,256]{3,2,1,0:T(8,128)} copy(f32[3,2,32,256]{3,2,1,0:T(8,128)S(1)} %window.1) | data formatting | bytes 393216

commit v4 on v3

--- a/solution.py
+++ b/solution.py
@@ -260,44 +260,53 @@
     inside = (u < 48) & (place >= 0) & (place < 32 * (last_xy + 1))
     select = jnp.where(inside & (l == 8 + 32 * core + u), 1.0, 0.0).astype(BF16)
 
-    for source in range(2):
-        if source == 1:
-            hand.wait()
-        tiles = strip[source].astype(F32).reshape(CHIPS, 2, 8, 128)
-        for q in range(2):
-            p = 2 * source + q
-            rows = tiles[:, q].reshape(256, 128).astype(BF16)
-            turned = dot_turned(select, rows)
-            for b, part in enumerate(neighbours(turned)):
-                vol[p, 64 * b : 64 * b + 64, :] = part.astype(BF16)
-            for chunk in range(2):
-                rows = slice(736 * chunk, 736 * chunk + 736)
-                found = dot(t1[rows, 0:192], vol[p])
-                if chunk == 0:
-                    found = relu_plus(found, b1, 32, low=7, keep_low=keep_low)
-                else:
-                    found = relu_plus(found, b1, 32, high=7, keep_high=keep_high)
-                for b, part in enumerate(neighbours(found)):
-                    one[p, b, rows, :] = part.astype(BF16)
-        for g in range(11):
-            for q in range(2):
-                p = 2 * source + q
-                field = jnp.concatenate([one[p, b, 128 * g : 128 * g + 192, :] for b in range(3)], axis=0)
-                found = relu_plus(dot(t2[...], field), b2, 32)
-                two[p, 128 * g : 128 * g + 128, :] = found.astype(BF16)
-                pairs = found.reshape(2, 2, 32, 256)
-                pairs = jnp.maximum(pairs[:, 0], pairs[:, 1]).reshape(64, 256)
-                pairs = jnp.maximum(pairs, pltpu.roll(pairs, 255, 1))
-                joined[p, 64 * g : 64 * g + 64, :] = pairs.astype(BF16)
-
     fine = iota((256, 128), 0)
     coarse = iota((256, 128), 1)
     pick = jnp.where(fine == 2 * coarse, 1.0, 0.0).astype(BF16)
-    for p in range(4):
+
+    def turn(source):
+        tiles = strip[source].astype(F32).reshape(CHIPS, 2, 8, 128)
+        for q in range(2):
+            turned = dot_turned(select, tiles[:, q].reshape(256, 128).astype(BF16))
+            for b, part in enumerate(neighbours(turned)):
+                vol[2 * source + q, 64 * b : 64 * b + 64, :] = part.astype(BF16)
+
+    def first_layer(p, start, stop):
+        rows = slice(32 * start, 32 * stop)
+        low, high = max(0, min(stop, 7) - start), max(0, stop - max(start, 39))
+        found = relu_plus(dot(t1[rows, 0:192], vol[p]), b1, 32, low, high, keep_low, keep_high)
+        for b, part in enumerate(neighbours(found)):
+            one[p, b, rows, :] = part.astype(BF16)
+
+    def second_layer(p, g):
+        field = jnp.concatenate([one[p, b, 128 * g : 128 * g + 192, :] for b in range(3)], axis=0)
+        found = relu_plus(dot(t2[...], field), b2, 32)
+        two[p, 128 * g : 128 * g + 128, :] = found.astype(BF16)
+        pairs = found.reshape(2, 2, 32, 256)
+        pairs = jnp.maximum(pairs[:, 0], pairs[:, 1]).reshape(64, 256)
+        pairs = jnp.maximum(pairs, pltpu.roll(pairs, 255, 1))
+        joined[p, 64 * g : 64 * g + 64, :] = pairs.astype(BF16)
+
+    def pool(p):
         found = dot(joined[p], pick)
         found = jnp.concatenate([found[:96] * keep_low, found[96:608], found[608:] * keep_high], axis=0).astype(BF16)
         t = jnp.where(core == 1, 2 * (p // 2), 2 - 2 * (p // 2)) + jnp.where(gz == 0, p % 2, 1 - p % 2)
         pooled[:, pl.ds(pl.multiple_of(128 * (t + 1), 128), 128)] = found
+
+    turn(0)
+    first_layer(0, 0, 23)
+    first_layer(0, 23, 46)
+    for p in range(1, 5):
+        for g in range(11):
+            second_layer(p - 1, g)
+            if p == 1 and g == 9:
+                hand.wait()
+                turn(1)
+            if p < 4:
+                first_layer(p, 4 * g, 4 * g + 4 if g < 10 else 46)
+            if p > 1 and g == 2:
+                pool(p - 2)
+    pool(3)
 
     mid[1024:1280, 0:128] = jnp.zeros((256, 128), BF16)
     for g in range(5):
@@ -375,7 +384,7 @@
 
     steps = [(g, t) for g in range(4) for t in range(2)]
     fields = []
-    for step in range(len(steps) + 2):
+    for step in range(len(steps) + 8):
         if step < len(steps):
             g, t = steps[step]
             parts = []
@@ -384,9 +393,9 @@
                 field = jnp.concatenate([dec[t, b, start : start + 192, :] for b in range(3)], axis=0)
                 parts.append(relu_plus(dot(tc[...], field), bc, 32).astype(BF16))
             fields.append(jnp.concatenate(parts, axis=0))
-        if step >= 2:
-            g, t = steps[step - 2]
-            found = jax.nn.sigmoid(dot(th[...], fields[step - 2]) + bh)
+        if step >= 8:
+            g, t = steps[step - 8]
+            found = jax.nn.sigmoid(dot(th[...], fields[step - 8]) + bh)
             s = jnp.where(gz == 0, t, 1 - t)
             for k in range(3):
                 out_ref[k, s, 8 * g : 8 * g + 8, :] = found[8 * k : 8 * k + 8]

time: 26.5 us -> 25.8 us (0.974)
  Pallas kernels: 25.6 us -> 25 us
    pallas_call x1, Pallas kernels: 25.6 us -> 25 us  [body(): pl.pallas_call(kernel, out_shape=pltpu.VMEM((3, 2, 32, 256), F32), in_spe...]
where the time goes in v4:
time: 25.8 us; the launch traced here: 25.7 us
  Pallas kernels  25 us (97%)
  local copies, waits for them, and re-layouts  0.68 us (3%)
    pallas_call x1, Pallas kernels, body(): pl.pallas_call(kernel, out_shape=pltpu.VMEM((3, 2, 32, 256), F32), in_spe...  25 us
    unnamed x1, local copies, waits for them, and re-layouts  0.68 us

profile of v4, /device:TPU:1, one launch (start us, length us, event | category | flops | bytes accessed | tf_op | source)
XLA Modules:
  0.0 25.7 jit_solution(18299055830223590843)
XLA Ops:
  0.0 25.0 %window.1 = f32[3,2,32,256]{3,2,1,0:T(8,128)S(1)} custom-call(bf16[2,4,2048]{2,1,0:T(4,128)(2,1)} %image_hbm.1, s32[2,4,2048]{2,1,0:T(4,128)} %crack_hbm.1, s32[2,4,2048]{2,1,0:T(4,128)} %fold_hbm.1, bf16[9,32]{1,0:T(8,128)(2,1)} %w1_hbm.1, f32[1,32]{1,0:T(1,128)} %bitcast.9, bf16[9,32,32]{2,1,0:T(8,128)(2,1)} %w2_hbm.1, f32[1,32]{1,0:T(1,128)} %bitcast.10, ...), custom_call_target="tpu_custom_call" | custom-call | tf_op jit(solution)/shard_map/window/pallas_call | solution.py:422
  25.0 0.7 %copy.19 = f32[3,2,32,256]{3,2,1,0:T(8,128)} copy(f32[3,2,32,256]{3,2,1,0:T(8,128)S(1)} %window.1) | data formatting | bytes 393216

commit v5 on v4

--- a/solution.py
+++ b/solution.py
@@ -195,9 +195,19 @@
         for b in range(3):
             col = column_of(w1[3 * a + b : 3 * a + b + 1])
             base[b // 2] = jnp.where(lane == 64 * (b % 2) + a, col, base[b // 2])
+    b1 = column_of(b1_ref[...])
+    bias = jnp.zeros((32, 128), F32)
+    rest = b1
+    for n in range(3):
+        part = rest.astype(BF16).astype(F32)
+        rest = rest - part
+        bias = jnp.where(lane == 64 + n, part, bias)
     for i in range(46):
+        pair = (pltpu.roll(base[0], i, 1), pltpu.roll(base[1], i, 1) + bias)
         for n in range(2):
-            t1[32 * i : 32 * i + 32, 128 * n : 128 * n + 128] = pltpu.roll(base[n], i, 1).astype(BF16)
+            moved = pair[n] * keep_low if i < 7 else pair[n] * keep_high if i >= 39 else pair[n]
+            t1[32 * i : 32 * i + 32, 128 * n : 128 * n + 128] = moved.astype(BF16)
+    vol[:, 192:208, :] = jnp.ones((4, 16, 256), BF16)
 
     plane_band(w2_ref, t2)
     plane_band(wc_ref, tc)
@@ -237,7 +247,6 @@
         heads = jnp.where(here, wide[k : k + 1], heads)
     th[...] = heads.astype(BF16)
 
-    b1 = column_of(b1_ref[...])
     b2 = column_of(b2_ref[...])
     bm = column_of(bm_ref[...])
     bd = column_of(bd_ref[...])
@@ -273,8 +282,7 @@
 
     def first_layer(p, start, stop):
         rows = slice(32 * start, 32 * stop)
-        low, high = max(0, min(stop, 7) - start), max(0, stop - max(start, 39))
-        found = relu_plus(dot(t1[rows, 0:192], vol[p]), b1, 32, low, high, keep_low, keep_high)
+        found = jnp.maximum(dot(t1[rows, 0:208], vol[p]), 0.0)
         for b, part in enumerate(neighbours(found)):
             one[p, b, rows, :] = part.astype(BF16)
 
@@ -415,7 +423,7 @@
         for shape in (
             (2, 16, 1024), (CHIPS, 16, 128), (2, CHIPS, 16, 128),
             (1472, 256), (128, 576), (384, 384), (384, 768), (128, 576), (128, 256), (24, 256),
-            (4, 192, 256), (4, 3, 1472, 256), (4, 1408, 256), (4, 704, 256), (704, 640), (1280, 512),
+            (4, 208, 256), (4, 3, 1472, 256), (4, 1408, 256), (4, 704, 256), (704, 640), (1280, 512),
             (1152, 256), (2, 576, 256), (2, 3, 1152, 256),
         )
     ]

time: 25.8 us -> 25.6 us (level)
  Pallas kernels: 25 us -> 24.7 us
    pallas_call x1, Pallas kernels: 25 us -> 24.7 us  [body(): pl.pallas_call(kernel, out_shape=pltpu.VMEM((3, 2, 32, 256), F32), in_spe...]
where the time goes in v5:
time: 25.6 us; the launch traced here: 25.4 us
  Pallas kernels  24.7 us (96%)
  local copies, waits for them, and re-layouts  0.68 us (3%)
    pallas_call x1, Pallas kernels, body(): pl.pallas_call(kernel, out_shape=pltpu.VMEM((3, 2, 32, 256), F32), in_spe...  24.7 us
    unnamed x1, local copies, waits for them, and re-layouts  0.68 us

profile of v5, /device:TPU:1, one launch (start us, length us, event | category | flops | bytes accessed | tf_op | source)
XLA Modules:
  0.0 25.4 jit_solution(174847789989850877)
XLA Ops:
  0.0 24.7 %window.1 = f32[3,2,32,256]{3,2,1,0:T(8,128)S(1)} custom-call(bf16[2,4,2048]{2,1,0:T(4,128)(2,1)} %image_hbm.1, s32[2,4,2048]{2,1,0:T(4,128)} %crack_hbm.1, s32[2,4,2048]{2,1,0:T(4,128)} %fold_hbm.1, bf16[9,32]{1,0:T(8,128)(2,1)} %w1_hbm.1, f32[1,32]{1,0:T(1,128)} %bitcast.9, bf16[9,32,32]{2,1,0:T(8,128)(2,1)} %w2_hbm.1, f32[1,32]{1,0:T(1,128)} %bitcast.10, ...), custom_call_target="tpu_custom_call" | custom-call | tf_op jit(solution)/shard_map/window/pallas_call | solution.py:430
  24.7 0.7 %copy.19 = f32[3,2,32,256]{3,2,1,0:T(8,128)} copy(f32[3,2,32,256]{3,2,1,0:T(8,128)S(1)} %window.1) | data formatting | bytes 393216
